TPU v7x, 32 devices: a whole 2x2x4 slice. The times are simulated.
32 devices in a mesh: groups: 2 (over y), samples: 4 (over z), snps: 4 (over x, core).
Axes of the slice: x: 2, y: 2, z: 4, core: 2. Of those that a mesh axis runs over, the one named last changes fastest.
Arguments:
- genotype: int32 [16384, 768], P(('groups', 'samples'), 'snps'), parts along dimension 0, may hold values from 0 to 170, as said below
- traits: bfloat16 [16384, 512], P(('groups', 'samples')), parts along dimension 0, may hold values from -6 to 6
- sample_mask: int32 [16384], P(('groups', 'samples')), parts along dimension 0, may hold values from 0 to 1
- block_ids: int32 [6144], P(('groups', 'snps')), parts along dimension 0, may hold values from 0 to 1, never falling along the last dimension, each value on 1 to 2304 neighbouring positions
- running_total: float32 [1024, 512], P(('groups', 'samples', 'snps')), parts along dimension 0, may hold values from -6 to 6
Outputs:
- assoc: float32 [4, 1536, 512], P('snps', ('groups', 'samples')), parts along dimension 1
- block_gram: float32 [2, 1024, 512], P(None, ('groups', 'samples', 'snps')), parts along dimension 1
- total: float32 [1024, 512], P(('groups', 'samples', 'snps')), parts along dimension 0
There are 2 independent parts, one for each index of `groups`. A program takes and returns all parts, laid end to end along the dimension named above; each array names one. Nothing has to cross between parts.
Inputs may be any that keep to these rules, and one draw needn't show every extreme that they name: `genotype`: each word holds 4 dosages of 0 to 2, SNP 4 w + f in bits 2 f and 2 f + 1 of word w; the pattern 3 never occurs. `block_ids`: never falling; each of the 2 blocks occurs.
All inputs are finite; a program needn't handle non-finite values.
Results may differ from a plain program's by a relative error of at most 0.0019.
Values may be sent and summed in bfloat16 or wider, within the bound.
A program may use at most 64 MiB of HBM per device.

v0:
```python
import math

import jax
import jax.numpy as jnp
from jax import lax
from jax.sharding import PartitionSpec as P

BLOCKS = 2


def unpack(words):
    shifts = 2 * lax.iota(jnp.int32, 4)
    values = words[:, :, None] >> shifts[None, None, :] & 3
    return values.reshape(words.shape[0], words.shape[1] * 4)


def shards(genotype, traits, sample_mask, block_ids, running_total):
    dosage = unpack(genotype).astype(jnp.bfloat16)
    keep = sample_mask.astype(jnp.bfloat16)
    masked = traits * keep[:, None]
    local_count = jnp.sum(sample_mask.astype(jnp.float32))
    local_colsum = jnp.dot(keep[None, :], traits, preferred_element_type=jnp.float32)[0]
    local_sums = jnp.dot(keep[None, :], dosage, preferred_element_type=jnp.float32)[0]
    local_squares = jnp.dot(keep[None, :], dosage * dosage, preferred_element_type=jnp.float32)[0]
    snp_count = dosage.shape[1]
    n_rows = snp_count // lax.axis_size("samples")
    offset = lax.axis_index("samples") * n_rows
    raw = lax.psum_scatter(
        lax.dot_general(
            dosage, masked, (((0,), (0,)), ((), ())), preferred_element_type=jnp.float32
        ),
        "samples",
        scatter_dimension=0,
        tiled=True,
    )
    count, colsum, sums, squares = lax.psum(
        (local_count, local_colsum, local_sums, local_squares), "samples"
    )
    sums = lax.dynamic_slice_in_dim(sums, offset, n_rows, 0)
    squares = lax.dynamic_slice_in_dim(squares, offset, n_rows, 0)
    mean = sums / count
    var = squares / count - mean * mean
    scale = lax.rsqrt((var + 1e-05) * count)
    assoc = (raw - mean[:, None] * colsum[None, :]) * scale[:, None]
    rounded = assoc.astype(jnp.bfloat16)
    factor = 1.0 / math.sqrt(snp_count * lax.axis_size("snps"))
    labels = lax.iota(jnp.int32, BLOCKS)
    own_ids = lax.dynamic_slice_in_dim(block_ids, offset, n_rows, 0)
    onehot = (labels[:, None] == own_ids[None, :]).astype(jnp.bfloat16)
    weighted = rounded[None, :, :] * onehot[:, :, None]
    partial_gram = jnp.einsum("brk,rl->bkl", weighted, rounded, preferred_element_type=jnp.float32)
    gram = lax.psum_scatter(partial_gram, ("samples", "snps"), scatter_dimension=1, tiled=True)
    block_gram = gram * factor
    total = running_total + jnp.sum(block_gram, axis=0)
    return (assoc[None, :, :], block_gram, total)


def solution(mesh):
    placed = (
        P(("groups", "samples"), "snps"),
        P(("groups", "samples"), None),
        P(("groups", "samples")),
        P(("groups", "snps")),
        P(("groups", "samples", "snps"), None),
    )
    return jax.shard_map(
        shards,
        mesh=mesh,
        in_specs=placed,
        out_specs=(
            P("snps", ("groups", "samples"), None),
            P(None, ("groups", "samples", "snps"), None),
            P(("groups", "samples", "snps"), None),
        ),
        check_vma=False,
    )
```

profile of v0, /device:TPU:0, one launch (start us, length us, event | category | flops | bytes accessed | tf_op | source)
XLA Modules:
  0.0 139.9 jit_solution(17681064325058127995)
XLA Ops:
  7.2 0.0 reduce-scatter.3.cloned.1.call-start
  7.2 5.9 %shift_right_arithmetic.24 = s32[2048,192,4]{0,2,1:T(4,128)} broadcast(s32[2048,192]{0,1:T(8,128)} %param.5), dimensions={0,1} | broadcast | bytes 7864320 | tf_op jit(solution)/shard_map/shift_right_arithmetic | solution.py:13
  13.1 0.0 copy-start.3
  13.1 7.6 %shift_right_arithmetic.25 = s32[2048,768]{0,1:T(8,128)} reshape(s32[2048,192,4]{0,2,1:T(4,128)} %shift_right_arithmetic.24) | data formatting | bytes 12582912 | tf_op jit(solution)/shard_map/shift_right_arithmetic | solution.py:13
  20.8 0.1 shift_right_arithmetic.27
  20.9 0.0 copy-done.3
  20.9 0.0 copy-start
  20.9 3.7 %and_convert_fusion = bf16[2048,768]{0,1:T(8,128)(2,1)S(1)} fusion(s32[2048,768]{0,1:T(8,128)} %shift_right_arithmetic.25, s32[768]{0:T(1024)S(1)} %shift_right_arithmetic.27), kind=kLoop, calls=%fused_computation | loop fusion | flops 4718592 | bytes 9440256 | tf_op jit(solution)/shard_map/convert_element_type | solution.py:18
  24.6 0.0 copy-done
  24.6 3.0 %fusion.2 = f32[768,512]{1,0:T(8,128)} fusion(bf16[2048,768]{0,1:T(8,128)(2,1)S(1)} %and_convert_fusion, bf16[2048,512]{1,0:T(8,128)(2,1)S(1)} %copy-done, bf16[2048]{0:T(1024)(128)(2,1)S(1)} %convert_element_type.24), kind=kOutput, calls=%fused_computation.3 | convolution fusion | flops 1611661312 | bytes 6819840 | tf_op jit(solution)/shard_map/dot_general | solution.py:29
  27.7 0.0 reduce-scatter.3.cloned.1.call-update
  27.7 0.0 reduce-scatter.5.cloned.1.call-start
  27.8 0.0 copy-start.1
  27.8 0.9 dynamic_slice.11
  28.7 0.6 convert_reduce_fusion
  29.3 0.9 convolution_reduce_fusion
  30.2 0.0 copy-done.1
  30.2 0.4 fusion.16
  30.6 0.9 fusion.4
  31.5 0.0 copy-start.2
  31.6 22.0 %all-reduce = (f32[768]{0:T(1024)S(1)}, f32[]{:T(128)}, f32[768]{0:T(1024)S(1)}, f32[512]{0:T(512)S(1)}) all-reduce(f32[768]{0:T(1024)S(1)} %convolution_reduce_fusion, f32[]{:T(128)} %convert_reduce_fusion, f32[768]{0:T(1024)S(1)} %fusion.4, f32[512]{0:T(512)S(1)} %bitcast.14), channel_id=1, replica_groups=mesh['groups'=2,'samples'=4,'snps'=4] {'samples'}, use_global_device_ids=true, to_apply=%region_1.0 | all-reduce | flops 2049 | bytes 16392 | tf_op jit(solution)/shard_map/psum | solution.py:36
  53.5 0.7 multiply_rsqrt_fusion
  54.3 11.9 %reduce-scatter.3.cloned.1.call-done = f32[192,512]{1,0:T(8,128)} async-done(((f32[768,512]{1,0:T(8,128)}), f32[192,512]{1,0:T(8,128)}) %reduce-scatter.3.cloned.1.call-update) | async-done | bytes 393232 | tf_op jit(solution)/shard_map/reduce_scatter | solution.py:28
  66.2 1.9 %fusion.10 = (bf16[192,512]{1,0:T(8,128)(2,1)S(1)}, f32[1,192,512]{2,1,0:T(8,128)}) fusion(f32[192,512]{1,0:T(8,128)} %reduce-scatter.3.cloned.1.call-done, f32[192]{0:T(256)S(1)} %get-tuple-element.9, f32[512]{0:T(512)S(1)} %get-tuple-element.6, f32[192]{0:T(256)S(1)} %get-tuple-element.10), kind=kLoop, calls=%fused_computation.11 | loop fusion | flops 393216 | bytes 986624 | tf_op jit(solution)/shard_map/convert_element_type | solution.py:45
  68.1 1.9 %fusion.8 = f32[2,512,512]{2,1,0:T(8,128)} fusion(bf16[192,512]{1,0:T(8,128)(2,1)S(1)} %get-tuple-element.11, bf16[2,192]{1,0:T(2,128)(2,1)S(1)} %compare_convert_fusion), kind=kOutput, calls=%fused_computation.8 | convolution fusion | flops 201523200 | bytes 2294528 | tf_op jit(solution)/shard_map/brk,rl->bkl/dot_general | solution.py:51
  70.0 0.0 reduce-scatter.5.cloned.1.call-update
  70.0 60.9 %reduce-scatter.5.cloned.1.call-done = f32[2,32,512]{2,1,0:T(8,128)} async-done(((f32[2,512,512]{2,1,0:T(8,128)}), f32[2,32,512]{2,1,0:T(8,128)}) %reduce-scatter.5.cloned.1.call-update) | async-done | bytes 131088 | tf_op jit(solution)/shard_map/reduce_scatter | solution.py:52
  130.9 1.6 %fusion.15 = (f32[32,512]{1,0:T(8,128)S(1)}, f32[2,32,512]{2,1,0:T(8,128)}) fusion(f32[2,32,512]{2,1,0:T(8,128)} %reduce-scatter.5.cloned.1.call-done), kind=kLoop, calls=%fused_computation.23 | loop fusion | flops 49152 | bytes 327680 | tf_op jit(solution)/shard_map/reduce_sum | solution.py:54
  132.4 0.0 copy-done.2
  132.4 0.6 add.29
  (5 shorter events, 0.0 us)
Async XLA Ops:
  7.2 59.0 %reduce-scatter.3.cloned.1.call-start = ((), (), s32[]{:S(2)}) async-start(), calls=%async_computation.2 | async-start | bytes 1966080 | tf_op jit(solution)/shard_map/reduce_scatter | solution.py:28
  13.1 7.8 %copy-start.3 = (s32[2048]{0:T(1024)S(1)}, s32[2048]{0:T(1024)}, u32[]{:S(2)}) copy-start(s32[2048]{0:T(1024)} %param.7) | copy-start | bytes 24580
  20.9 3.7 %copy-start = (bf16[2048,512]{1,0:T(8,128)(2,1)S(1)}, bf16[2048,512]{1,0:T(8,128)(2,1)}, u32[]{:S(2)}) copy-start(bf16[2048,512]{1,0:T(8,128)(2,1)} %param.6) | copy-start | bytes 6291460
  27.7 103.2 %reduce-scatter.5.cloned.1.call-start = ((), (), s32[]{:S(2)}) async-start(), calls=%async_computation.3 | async-start | bytes 2228224 | tf_op jit(solution)/shard_map/reduce_scatter | solution.py:52
  27.8 2.5 %copy-start.1 = (bf16[2048,512]{1,0:T(8,128)(2,1)S(1)}, bf16[2048,512]{1,0:T(8,128)(2,1)}, u32[]{:S(2)}) copy-start(bf16[2048,512]{1,0:T(8,128)(2,1)} %param.6) | copy-start | bytes 6291460
  31.5 100.9 %copy-start.2 = (f32[32,512]{1,0:T(8,128)S(1)}, f32[32,512]{1,0:T(8,128)}, u32[]{:S(2)}) copy-start(f32[32,512]{1,0:T(8,128)} %param.9) | copy-start | bytes 196612
Sparse Core Ops, SparseCore 0:
  27.8 38.3 reduce-scatter.2
  70.1 60.6 reduce-scatter.4
where the time goes:
time: 140 us
  waiting for transfers between devices  72.8 us (52%)
  blocking collectives  22 us (16%)
  local copies, waits for them, and re-layouts  14.6 us (10%)
  between operations  14.1 us (10%)
  other arithmetic  9.14 us (7%)
  matrix products  7.2 us (5%)
    reduce_scatter x1, waiting for transfers between devices, shards(): lax.psum_scatter(partial_gram, ('samples', 'snps'), scatter_dimension=1,...  60.9 us
    psum x1, blocking collectives, shards(): lax.psum((local_count, local_colsum, local_sums, local_squares), 'samples')  22 us
    shift_right_arithmetic x4, local copies, waits for them, and re-layouts, unpack(): values = words[:, :, None] >> shifts[None, None, :] & 3  13.6 us
    reduce_scatter x1, waiting for transfers between devices, shards(): lax.psum_scatter(lax.dot_general(dosage, masked, (((0,), (0,)), ((), ()))...  11.9 us
    convert_element_type x1, other arithmetic, shards(): dosage = unpack(genotype).astype(jnp.bfloat16)  3.71 us
    dot_general x1, matrix products, shards(): lax.dot_general(dosage, masked, (((0,), (0,)), ((), ())), preferred_eleme...  3.04 us
  transfers between devices with their start and end apart: 2, of which 2 were waited for; matrix products, arithmetic and copies ran while one was open for 3% of the time, Pallas kernels for 0%

commit v1 on v0

--- a/solution.py
+++ b/solution.py
@@ -1,8 +1,11 @@
+import functools
 import math
 
 import jax
 import jax.numpy as jnp
 from jax import lax
+from jax.experimental import pallas as pl
+from jax.experimental.pallas import tpu as pltpu
 from jax.sharding import PartitionSpec as P
 
 BLOCKS = 2
@@ -55,6 +58,233 @@
     return (assoc[None, :, :], block_gram, total)
 
 
+MESH = pl.DeviceIdType.MESH
+F32 = jnp.float32
+
+
+def kernel(
+    n_snp_dev, factor, geno, traits, mask, ids, running, assoc, gram, total,
+    words, lhs, y_own, q_send, q_recv, st_send, st_recv, z_buf, zt, mixed, g_own, g_send, g_recv,
+    q_ss, q_rs, st_ss, st_rs, z_ss, z_rs, g_ss, g_rs,
+):
+    grp, s, p = (lax.axis_index(a) for a in ("groups", "samples", "snps"))
+    ns = lax.axis_size("samples")
+    n_samples, n_words = geno.shape
+    wpd = n_words // ns
+    rows = 4 * wpd
+    traits_n = traits.shape[1]
+
+    def along(k):
+        return (grp, lax.rem(s + k, ns), p)
+
+    def other(bit):
+        return (grp, s, p + bit - 2 * bit * lax.rem(p // bit, 2))
+
+    barrier = pltpu.get_barrier_semaphore()
+    peers = [along(k) for k in range(1, ns)] + [other(1), other(2)]
+    for peer in peers:
+        pl.semaphore_signal(barrier, inc=1, device_id=peer, device_id_type=MESH)
+
+    for i in range(n_samples // 128):
+        block = geno[i * 128:(i + 1) * 128, :]
+        block = jnp.concatenate([block, jnp.zeros((128, -n_words % 128), jnp.int32)], axis=1)
+        words[:, i * 128:(i + 1) * 128] = block.T[:n_words] * mask[:, i * 128:(i + 1) * 128]
+    count = jnp.sum(mask[...].astype(F32), axis=1, keepdims=True)
+    lhs[rows:rows + 16, :] = jnp.broadcast_to(mask[...].astype(F32), (16, n_samples)).astype(jnp.bfloat16)
+
+    pl.semaphore_wait(barrier, len(peers))
+
+    def q_copy(k):
+        return pltpu.make_async_remote_copy(
+            q_send.at[k - 1], q_recv.at[k - 1], q_ss.at[k - 1], q_rs.at[k - 1],
+            device_id=along(k), device_id_type=MESH)
+
+    def st_copy(k):
+        return pltpu.make_async_remote_copy(
+            st_send.at[k - 1], st_recv.at[k - 1], st_ss.at[k - 1], st_rs.at[k - 1],
+            device_id=along(k), device_id_type=MESH)
+
+    lane = lax.broadcasted_iota(jnp.int32, (rows, 128), 1)
+    sub = lax.broadcasted_iota(jnp.int32, (8, traits_n), 0)
+
+    def one(k, carry):
+        t = lax.rem(s + k, ns)
+        w = words[pl.ds(pl.multiple_of(t * wpd, wpd), wpd), :]
+        s1, s2 = [], []
+        for f in range(4):
+            d = ((w >> (2 * f)) & 3).astype(F32)
+            s1.append(jnp.sum(d, axis=1, keepdims=True))
+            s2.append(jnp.sum(d * d, axis=1, keepdims=True))
+            lhs[f * wpd:(f + 1) * wpd, :] = d.astype(jnp.bfloat16)
+        sums = jnp.concatenate(s1, axis=0)
+        squares = jnp.concatenate(s2, axis=0)
+        raw = jnp.dot(lhs[...], traits[...], preferred_element_type=F32)
+        colsum = raw[rows:rows + 1]
+        y = raw[:rows] - (sums / jnp.maximum(count, 1.0)) * colsum
+        top = jnp.maximum(jnp.max(jnp.abs(y), axis=1, keepdims=True), 1e-30)
+        y_own[...] = y
+        q_send[k - 1] = jnp.round(y * (32767.0 / top)).astype(jnp.int32).astype(jnp.int16)
+        cols = jnp.where(lane == 0, sums, jnp.where(lane == 1, squares, jnp.where(lane == 2, top * (1.0 / 32767.0), 0.0)))
+        cols = jnp.concatenate([cols, jnp.zeros((-rows % 128, 128), F32)], axis=0).T[:8]
+        cols = jnp.concatenate([cols, jnp.zeros((8, traits_n - cols.shape[1]), F32)], axis=1)
+        st_send[k - 1] = jnp.where(sub == 3, colsum, jnp.where(sub == 4, count, cols))
+
+        @pl.when(k < ns)
+        def _():
+            st_copy(k).start()
+            q_copy(k).start()
+
+        return carry
+
+    lax.fori_loop(1, ns + 1, one, 0)
+
+    padded = rows + (-rows % 128)
+
+    def columns(st):
+        tall = jnp.concatenate([st[:, :padded], jnp.zeros((120, padded), F32)], axis=0).T
+        return tall[:rows, 0:1], tall[:rows, 1:2], tall[:rows, 2:3]
+
+    own = st_send[ns - 1]
+    parts = [(own, columns(own))]
+    y = y_own[...]
+    for k in range(1, ns):
+        st_copy(k).wait_recv()
+        st = st_recv[k - 1]
+        cols = columns(st)
+        parts.append((st, cols))
+        q_copy(k).wait_recv()
+        y = y + q_recv[k - 1].astype(jnp.int32).astype(F32) * cols[2]
+    n = sum(st[4:5, 0:1] for st, _ in parts)
+    mean = sum(c[0] for _, c in parts) / n
+    var = sum(c[1] for _, c in parts) / n - mean * mean
+    scale = lax.rsqrt((var + 1e-05) * n)
+    for st, c in parts:
+        y = y + (c[0] / jnp.maximum(st[4:5, 0:1], 1.0) - mean) * st[3:4]
+    z = y * scale
+    zb = z.astype(jnp.bfloat16)
+    z_buf[0, 0:rows, :] = zb
+    n0 = jnp.sum((ids[...] == 0).astype(F32), axis=1, keepdims=True)
+    at = lax.broadcasted_iota(jnp.int32, (1, traits_n), 1)
+    field = sum((at >= f * wpd).astype(jnp.int32) for f in range(1, 4))
+    j = s * rows + 4 * (at - field * wpd) + field
+    first = (j.astype(F32) < n0).astype(F32)
+    z_buf[0, rows:rows + 16, :] = jnp.broadcast_to(first, (16, traits_n)).astype(jnp.bfloat16)
+
+    def z_copy(src, dst, to):
+        return pltpu.make_async_remote_copy(
+            z_buf.at[src], z_buf.at[dst], z_ss.at[dst - 1], z_rs.at[dst - 1],
+            device_id=to, device_id_type=MESH)
+
+    far, near, relay = z_copy(0, 2, other(2)), z_copy(0, 1, other(1)), z_copy(2, 3, other(1))
+    far.start()
+    near.start()
+    for c in range(traits_n // 128):
+        for f in range(4):
+            mixed[c, pl.ds(f, wpd, stride=4), :] = z[f * wpd:(f + 1) * wpd, c * 128:(c + 1) * 128]
+        assoc[:, c * 128:(c + 1) * 128] = mixed[c]
+
+    own_rows = running.shape[0]
+
+    def gram_of(i, acc):
+        zc = z_buf[i, 0:rows, :]
+        zc = jnp.concatenate([zc, jnp.zeros((padded - rows, traits_n), jnp.bfloat16)], axis=0)
+        zt[...] = zc.astype(F32).T
+        left = [zt[pl.ds(pl.multiple_of((lax.rem(s + k, ns) * n_snp_dev + p) * own_rows, own_rows), own_rows), :] for k in range(1, ns + 1)]
+        left = jnp.concatenate(left, axis=0)
+        chosen = z_buf[i, rows:rows + 16, :].astype(F32)[0:1, :padded]
+        both = jnp.concatenate([left * chosen, left * (1.0 - chosen)], axis=0).astype(jnp.bfloat16)
+        new = jnp.dot(both, zc, preferred_element_type=F32)
+        return new if acc is None else acc + new
+
+    acc = gram_of(0, None)
+    near.wait_recv()
+    acc = gram_of(1, acc)
+    far.wait_recv()
+    relay.start()
+    acc = gram_of(2, acc)
+    relay.wait_recv()
+    acc = gram_of(3, acc)
+
+    def g_copy(k):
+        return pltpu.make_async_remote_copy(
+            g_send.at[k - 1], g_recv.at[k - 1], g_ss.at[k - 1], g_rs.at[k - 1],
+            device_id=along(k), device_id_type=MESH)
+
+    half = ns * own_rows
+    for k in range(1, ns):
+        for b in range(BLOCKS):
+            lo = b * half + (k - 1) * own_rows
+            g_send[k - 1, b] = acc[lo:lo + own_rows].astype(jnp.bfloat16)
+        g_copy(k).start()
+    for b in range(BLOCKS):
+        lo = b * half + (ns - 1) * own_rows
+        g_own[b] = acc[lo:lo + own_rows]
+    out = g_own[...]
+    for k in range(1, ns):
+        g_copy(k).wait_recv()
+        out = out + g_recv[k - 1].astype(F32)
+    out = out * factor
+    gram[...] = out
+    total[...] = running[...] + (out[0] + out[1])
+    for k in range(1, ns):
+        q_copy(k).wait_send()
+        st_copy(k).wait_send()
+        g_copy(k).wait_send()
+    for c in (far, near, relay):
+        c.wait_send()
+
+
+def fused(genotype, traits, sample_mask, block_ids, running_total):
+    ns, np_ = lax.axis_size("samples"), lax.axis_size("snps")
+    n_samples, n_words = genotype.shape
+    k = traits.shape[1]
+    rows = 4 * n_words // ns
+    padded = rows + (-rows % 128)
+    own = running_total.shape[0]
+    factor = 1.0 / math.sqrt(4 * n_words * np_)
+    vmem = pl.BlockSpec(memory_space=pltpu.VMEM)
+    bf16, dma = jnp.bfloat16, pltpu.SemaphoreType.DMA
+    assoc, gram, total = pl.pallas_call(
+        functools.partial(kernel, np_, factor),
+        out_shape=(
+            jax.ShapeDtypeStruct((rows, k), F32),
+            jax.ShapeDtypeStruct((BLOCKS, own, k), F32),
+            jax.ShapeDtypeStruct((own, k), F32),
+        ),
+        in_specs=[vmem] * 5,
+        out_specs=(vmem,) * 3,
+        scratch_shapes=[
+            pltpu.VMEM((n_words, n_samples), jnp.int32),
+            pltpu.VMEM((rows + 16, n_samples), bf16),
+            pltpu.VMEM((rows, k), F32),
+            pltpu.VMEM((ns, rows, k), jnp.int16),
+            pltpu.VMEM((ns - 1, rows, k), jnp.int16),
+            pltpu.VMEM((ns, 8, k), F32),
+            pltpu.VMEM((ns - 1, 8, k), F32),
+            pltpu.VMEM((np_, rows + 16, k), bf16),
+            pltpu.VMEM((k, padded), F32),
+            pltpu.VMEM((k // 128, rows, 128), F32),
+            pltpu.VMEM((BLOCKS, own, k), F32),
+            pltpu.VMEM((ns - 1, BLOCKS, own, k), bf16),
+            pltpu.VMEM((ns - 1, BLOCKS, own, k), bf16),
+        ] + [dma((ns - 1,))] * 4 + [dma((3,))] * 2 + [dma((ns - 1,))] * 2,
+        compiler_params=pltpu.CompilerParams(
+            collective_id=0, has_side_effects=True, vmem_limit_bytes=48 * 1024 * 1024
+        ),
+    )(genotype, traits, sample_mask.reshape(1, -1), block_ids.reshape(1, -1), running_total)
+    return assoc[None], gram, total
+
+
+def body(genotype, traits, sample_mask, block_ids, running_total):
+    args = (genotype, traits, sample_mask, block_ids, running_total)
+    ns = lax.axis_size("samples")
+    n_words = genotype.shape[1]
+    whole_tiles = n_words % (16 * ns) == 0 and running_total.shape[0] % 32 == 0
+    if lax.axis_size("snps") == 4 and 1 < ns <= 4 and whole_tiles and 4 * n_words // ns <= traits.shape[1]:
+        return fused(*args)
+    return shards(*args)
+
+
 def solution(mesh):
     placed = (
         P(("groups", "samples"), "snps"),
@@ -64,7 +294,7 @@
         P(("groups", "samples", "snps"), None),
     )
     return jax.shard_map(
-        shards,
+        body,
         mesh=mesh,
         in_specs=placed,
         out_specs=(

time: 140 us -> 45.6 us (0.33)
  waiting for transfers between devices: 72.8 us -> 0 us
  Pallas kernels: 0 us -> 38.5 us
  blocking collectives: 22 us -> 0 us
  between operations: 14.1 us -> 0.69 us
  other arithmetic: 9.14 us -> 0 us
  local copies, waits for them, and re-layouts: 14.6 us -> 6.18 us
  matrix products: 7.2 us -> 0 us
    reduce_scatter x2 -> x0, waiting for transfers between devices: 72.8 us -> none  [the longest x1 60.9 us: shards(): lax.psum_scatter(partial_gram, ('samples', 'snps'), scatter_dimension=1,...]
    pallas_call x0 -> x1, Pallas kernels: none -> 38.5 us  [fused(): pl.pallas_call(functools.partial(kernel, np_, factor), out_shape=(jax.Sha...]
    psum x1 -> x0, blocking collectives: 22 us -> none  [shards(): lax.psum((local_count, local_colsum, local_sums, local_squares), 'samples')]
    shift_right_arithmetic x4 -> x0, local copies, waits for them, and re-layouts: 13.6 us -> none  [unpack(): values = words[:, :, None] >> shifts[None, None, :] & 3]
    dot_general x5 -> x0, matrix products: 7.2 us -> none  [the longest x1 3.04 us: shards(): lax.dot_general(dosage, masked, (((0,), (0,)), ((), ())), preferred_eleme...]
    convert_element_type x4 -> x0, other arithmetic: 5.6 us -> none  [the longest x1 3.71 us: shards(): dosage = unpack(genotype).astype(jnp.bfloat16)]
    unnamed x8 -> x10, local copies, waits for them, and re-layouts: 0.02 us -> 5.46 us
    reduce_sum x2 -> x0, other arithmetic: 2.18 us -> none  [the longest x1 1.58 us: shards(): total = running_total + jnp.sum(block_gram, axis=0)]
  transfers between devices with their start and end apart: 2 -> 0, of which waited for: 2 -> 0; matrix products, arithmetic and copies ran while one was open for 3% -> 0% of each run, Pallas kernels for 0% -> 0%
where the time goes in v1:
time: 45.6 us; the launch traced here: 45.4 us
  Pallas kernels  38.5 us (84%)
  local copies, waits for them, and re-layouts  6.18 us (14%)
  between operations  0.69 us (2%)
    pallas_call x1, Pallas kernels, fused(): pl.pallas_call(functools.partial(kernel, np_, factor), out_shape=(jax.Sha...  38.5 us
    unnamed x10, local copies, waits for them, and re-layouts  5.46 us

profile of v1, /device:TPU:0, one launch (start us, length us, event | category | flops | bytes accessed | tf_op | source)
XLA Modules:
  0.0 45.4 jit_solution(15522889097834460818)
XLA Ops:
  0.6 0.0 copy-start.1
  0.6 0.0 copy-start.2
  0.7 0.7 %reshape.13.ids = s32[1,768]{1,0:T(1,128)S(1)} reshape(s32[768]{0:T(1024)} %param.8) | data formatting | bytes 6144 | tf_op jit(solution)/shard_map/reshape | solution.py:274
  1.4 1.8 %copy.8.geno = s32[2048,192]{1,0:T(8,128)S(1)} copy(s32[2048,192]{0,1:T(8,128)} %param.5) | data formatting | bytes 3145728 | tf_op args[0]
  3.2 0.0 copy-done.1
  3.2 0.0 copy-done.2
  3.2 0.0 copy-start
  3.2 1.6 %copy-done = bf16[2048,512]{1,0:T(8,128)(2,1)S(1)} copy-done((bf16[2048,512]{1,0:T(8,128)(2,1)S(1)}, bf16[2048,512]{1,0:T(8,128)(2,1)}, u32[]{:S(2)}) %copy-start) | copy-done | bytes 2097176
  4.8 38.5 %shard_map.76 = (f32[192,512]{1,0:T(8,128)S(1)}, f32[2,32,512]{2,1,0:T(8,128)S(1)}, f32[32,512]{1,0:T(8,128)S(1)}) custom-call(s32[2048,192]{1,0:T(8,128)S(1)} %copy.8.geno, bf16[2048,512]{1,0:T(8,128)(2,1)S(1)} %copy-done, s32[1,2048]{1,0:T(1,128)S(1)} %bitcast.3, s32[1,768]{1,0:T(1,128)S(1)} %reshape.13.ids, f32[32,512]{1,0:T(8,128)S(1)} %copy-done.1), custom_call_target="tpu_custom_call" | custom-call | tf_op jit(solution)/shard_map/pallas_call | solution.py:247
  43.3 0.7 %copy.12 = f32[1,192,512]{2,1,0:T(8,128)} copy(f32[1,192,512]{2,1,0:T(8,128)S(1)} %bitcast.2) | data formatting | bytes 786432
  44.1 0.7 %copy.13 = f32[2,32,512]{2,1,0:T(8,128)} copy(f32[2,32,512]{2,1,0:T(8,128)S(1)} %get-tuple-element.13) | data formatting | bytes 262144
  44.7 0.6 %copy.14 = f32[32,512]{1,0:T(8,128)} copy(f32[32,512]{1,0:T(8,128)S(1)} %get-tuple-element.14) | data formatting | bytes 131072
Async XLA Ops:
  0.6 2.6 %copy-start.1 = (f32[32,512]{1,0:T(8,128)S(1)}, f32[32,512]{1,0:T(8,128)}, u32[]{:S(2)}) copy-start(f32[32,512]{1,0:T(8,128)} %running.1) | copy-start | bytes 196612
  0.6 2.6 %copy-start.2 = (s32[2048]{0:T(1024)S(1)}, s32[2048]{0:T(1024)}, u32[]{:S(2)}) copy-start(s32[2048]{0:T(1024)} %param.7) | copy-start | bytes 24580
  3.2 1.6 %copy-start = (bf16[2048,512]{1,0:T(8,128)(2,1)S(1)}, bf16[2048,512]{1,0:T(8,128)(2,1)}, u32[]{:S(2)}) copy-start(bf16[2048,512]{1,0:T(8,128)(2,1)} %traits.1) | copy-start | bytes 6291460

commit v2 on v0

--- a/solution.py
+++ b/solution.py
@@ -1,8 +1,11 @@
+import functools
 import math
 
 import jax
 import jax.numpy as jnp
 from jax import lax
+from jax.experimental import pallas as pl
+from jax.experimental.pallas import tpu as pltpu
 from jax.sharding import PartitionSpec as P
 
 BLOCKS = 2
@@ -55,6 +58,292 @@
     return (assoc[None, :, :], block_gram, total)
 
 
+MESH = pl.DeviceIdType.MESH
+F32 = jnp.float32
+BF16 = jnp.bfloat16
+PW = 16
+PR = 4 * PW
+
+
+def kernel(
+    n_snp_dev, factor, geno, traits_hbm, mask, ids, running, assoc, gram, total,
+    words, traits, lhs, y_own, q_send, q_recv, st_send, st_recv, n_buf, z_buf, zt, mixed, g_own, g_send, g_recv,
+    in_sem, q_ss, q_rs, st_ss, st_rs, n_ss, n_rs, z_ss, z_rs, g_ss, g_rs,
+):
+    grp, s, p = (lax.axis_index(a) for a in ("groups", "samples", "snps"))
+    ns = lax.axis_size("samples")
+    n_words, n_samples = words.shape
+    wpd = n_words // ns
+    pieces = wpd // PW
+    rows = 4 * wpd
+    width = traits.shape[1]
+
+    geno_in = pltpu.make_async_copy(geno, words, in_sem.at[0])
+    traits_in = pltpu.make_async_copy(traits_hbm, traits, in_sem.at[1])
+    geno_in.start()
+    traits_in.start()
+
+    def along(k):
+        return (grp, lax.rem(s + k, ns), p)
+
+    def flip(bit):
+        return bit - 2 * bit * lax.rem(p // bit, 2)
+
+    def other(x):
+        return (grp, s, p + sum(flip(b) for b in (1, 2) if x & b))
+
+    barrier = pltpu.get_barrier_semaphore()
+    peers = [along(k) for k in range(1, ns)] + [other(x) for x in range(1, 4)]
+    for peer in peers:
+        pl.semaphore_signal(barrier, inc=1, device_id=peer, device_id_type=MESH)
+
+    keep = mask[...]
+    count = jnp.sum(keep.astype(F32), axis=1, keepdims=True)
+    lhs[ns * PR:, :] = jnp.broadcast_to(keep.astype(F32), (16, n_samples)).astype(BF16)
+    n0 = jnp.sum((ids[...] == 0).astype(F32), axis=1, keepdims=True)
+    n_buf[0] = jnp.broadcast_to(n0, n_buf.shape[1:])
+
+    def remote(src, dst, ss, rs, to):
+        return pltpu.make_async_remote_copy(src, dst, ss, rs, device_id=to, device_id_type=MESH)
+
+    def q_copy(c, k):
+        return remote(q_send.at[c, k - 1], q_recv.at[c, k - 1], q_ss.at[c, k - 1], q_rs.at[c, k - 1], along(k))
+
+    def st_copy(c, k):
+        return remote(st_send.at[c, k - 1], st_recv.at[c, k - 1], st_ss.at[c, k - 1], st_rs.at[c, k - 1], along(k))
+
+    def n_copy(x):
+        return remote(n_buf.at[0], n_buf.at[x], n_ss.at[x - 1], n_rs.at[x - 1], other(x))
+
+    def z_copy(c, src, dst, x):
+        return remote(
+            z_buf.at[c, pl.ds(src * PR, PR)], z_buf.at[c, pl.ds(dst * PR, PR)],
+            z_ss.at[c, dst - 1], z_rs.at[c, dst - 1], other(x))
+
+    def far(c):
+        return z_copy(c, 0, 2, 2)
+
+    def near(c):
+        return z_copy(c, 0, 1, 1)
+
+    def relay(c):
+        return z_copy(c, 2, 3, 1)
+
+    def g_copy(k):
+        return remote(g_send.at[k - 1], g_recv.at[k - 1], g_ss.at[k - 1], g_rs.at[k - 1], along(k))
+
+    pl.semaphore_wait(barrier, len(peers))
+    for x in range(1, 4):
+        n_copy(x).start()
+    geno_in.wait()
+    lane = lax.broadcasted_iota(jnp.int32, (PR, 128), 1)
+    sub = lax.broadcasted_iota(jnp.int32, (8, 128), 0)
+
+    def one(c, carry):
+        stats = []
+        for k in range(1, ns + 1):
+            t = lax.rem(s + k, ns)
+            w = words[pl.ds(pl.multiple_of(t * wpd + c * PW, PW), PW), :] * keep
+            s1, s2 = [], []
+            for f in range(4):
+                d = ((w >> (2 * f)) & 3).astype(F32)
+                s1.append(jnp.sum(d, axis=1, keepdims=True))
+                s2.append(jnp.sum(d * d, axis=1, keepdims=True))
+                at = (k - 1) * PR + f * PW
+                lhs[at:at + PW, :] = d.astype(BF16)
+            stats.append((jnp.concatenate(s1, axis=0), jnp.concatenate(s2, axis=0)))
+
+        @pl.when(c == 0)
+        def _():
+            traits_in.wait()
+
+        raw = jnp.dot(lhs[...], traits[...], preferred_element_type=F32)
+        colsum = raw[ns * PR:ns * PR + 1]
+        tail = jnp.concatenate(
+            [jnp.zeros((3, 128), F32)] + [colsum[:, i * 128:(i + 1) * 128] for i in range(4)]
+            + [jnp.broadcast_to(count, (1, 128))], axis=0)
+        for k in range(1, ns + 1):
+            sums, squares = stats[k - 1]
+            y = raw[(k - 1) * PR:k * PR] - (sums / jnp.maximum(count, 1.0)) * colsum
+            top = jnp.maximum(jnp.max(jnp.abs(y), axis=1, keepdims=True), 1e-30)
+            if k < ns:
+                q_send[c, k - 1] = jnp.round(y * (32767.0 / top)).astype(jnp.int32).astype(jnp.int16)
+            else:
+                y_own[c] = y
+            cols = jnp.where(lane == 0, sums, jnp.where(lane == 1, squares, top * (1.0 / 32767.0)))
+            cols = jnp.concatenate([cols, jnp.zeros((128 - PR, 128), F32)], axis=0).T[:8]
+            st_send[c, k - 1] = jnp.where(sub < 3, cols, tail)
+            if k < ns:
+                st_copy(c, k).start()
+                q_copy(c, k).start()
+        return carry
+
+    lax.fori_loop(0, pieces, one, 0)
+
+    def columns(st):
+        tall = jnp.concatenate([st, jnp.zeros((120, 128), F32)], axis=0).T
+        return tall[:PR, 0:1], tall[:PR, 1:2], tall[:PR, 2:3]
+
+    def standardise(c):
+        st = st_send[c, ns - 1]
+        parts = [(st, columns(st))]
+        y = y_own[c]
+        for k in range(1, ns):
+            st_copy(c, k).wait_recv()
+            st = st_recv[c, k - 1]
+            cols = columns(st)
+            parts.append((st, cols))
+            q_copy(c, k).wait_recv()
+            y = y + q_recv[c, k - 1].astype(jnp.int32).astype(F32) * cols[2]
+        n = sum(st[7:8, 0:1] for st, _ in parts)
+        mean = sum(cols[0] for _, cols in parts) / n
+        var = sum(cols[1] for _, cols in parts) / n - mean * mean
+        scale = lax.rsqrt((var + 1e-05) * n)
+        for st, cols in parts:
+            colsum = jnp.concatenate([st[i:i + 1] for i in range(3, 7)], axis=1)
+            y = y + (cols[0] / jnp.maximum(st[7:8, 0:1], 1.0) - mean) * colsum
+        z = y * scale
+        z_buf[c, 0:PR, :] = z.astype(BF16)
+        far(c).start()
+        near(c).start()
+        for i in range(width // 128):
+            for f in range(4):
+                mixed[i, pl.ds(c * PR + f, PW, stride=4), :] = z[f * PW:(f + 1) * PW, i * 128:(i + 1) * 128]
+            assoc[c * PR:(c + 1) * PR, i * 128:(i + 1) * 128] = mixed[i, c * PR:(c + 1) * PR, :]
+
+    own_rows = running.shape[0]
+    lanes = lax.broadcasted_iota(jnp.int32, (1, 4 * PR), 1)
+    slot = lanes // PR
+    snp = s * rows + 4 * lax.rem(lanes, PW) + lax.rem(lanes, PR) // PW
+
+    def limits():
+        for x in range(1, 4):
+            n_copy(x).wait_recv()
+        return sum(jnp.where(slot == x, n_buf[x, 0:1, 0:1], 0.0) for x in range(4))
+
+    def gram_of(c, limit):
+        near(c).wait_recv()
+        relay(c).wait_recv()
+        zc = z_buf[c]
+        zt[...] = zc.astype(F32).T
+        left = jnp.concatenate([
+            zt[pl.ds(pl.multiple_of((lax.rem(s + k, ns) * n_snp_dev + p) * own_rows, own_rows), own_rows), :]
+            for k in range(1, ns + 1)], axis=0)
+        chosen = ((snp + c * PR).astype(F32) < limit).astype(F32)
+        both = jnp.concatenate([left * chosen, left * (1.0 - chosen)], axis=0).astype(BF16)
+        return jnp.dot(both, zc, preferred_element_type=F32)
+
+    acc, limit = 0.0, None
+    for c in range(pieces):
+        standardise(c)
+        if c >= 1:
+            far(c - 1).wait_recv()
+            relay(c - 1).start()
+        if c >= 2:
+            limit = limits() if limit is None else limit
+            acc = acc + gram_of(c - 2, limit)
+    far(pieces - 1).wait_recv()
+    relay(pieces - 1).start()
+    limit = limits() if limit is None else limit
+    for c in range(max(pieces - 2, 0), pieces):
+        acc = acc + gram_of(c, limit)
+
+    half = ns * own_rows
+    for k in range(1, ns):
+        for b in range(BLOCKS):
+            lo = b * half + (k - 1) * own_rows
+            g_send[k - 1, b] = acc[lo:lo + own_rows].astype(BF16)
+        g_copy(k).start()
+    for b in range(BLOCKS):
+        lo = b * half + (ns - 1) * own_rows
+        g_own[b] = acc[lo:lo + own_rows]
+    out = g_own[...]
+    for k in range(1, ns):
+        g_copy(k).wait_recv()
+        out = out + g_recv[k - 1].astype(F32)
+    out = out * factor
+    gram[...] = out
+    total[...] = running[...] + (out[0] + out[1])
+    for c in range(pieces):
+        for k in range(1, ns):
+            q_copy(c, k).wait_send()
+            st_copy(c, k).wait_send()
+        for copy in (far(c), near(c), relay(c)):
+            copy.wait_send()
+    for k in range(1, ns):
+        g_copy(k).wait_send()
+    for x in range(1, 4):
+        n_copy(x).wait_send()
+
+
+def store(*refs):
+    n = len(refs) // 2
+    sems = refs[-1]
+    copies = [pltpu.make_async_copy(refs[i], refs[n + i], sems.at[i]) for i in range(n)]
+    for copy in copies:
+        copy.start()
+    for copy in copies:
+        copy.wait()
+
+
+def fused(genotype, traits, sample_mask, block_ids, running_total):
+    ns, np_ = lax.axis_size("samples"), lax.axis_size("snps")
+    n_samples, n_words = genotype.shape
+    k = traits.shape[1]
+    rows = 4 * n_words // ns
+    pieces = rows // PR
+    own = running_total.shape[0]
+    factor = 1.0 / math.sqrt(4 * n_words * np_)
+    vmem = pl.BlockSpec(memory_space=pltpu.VMEM)
+    hbm = pl.BlockSpec(memory_space=pltpu.HBM)
+    dma = pltpu.SemaphoreType.DMA
+    shapes = (
+        jax.ShapeDtypeStruct((rows, k), F32),
+        jax.ShapeDtypeStruct((BLOCKS, own, k), F32),
+        jax.ShapeDtypeStruct((own, k), F32),
+    )
+    results = pl.pallas_call(
+        functools.partial(kernel, np_, factor),
+        out_shape=shapes,
+        in_specs=[hbm, hbm, vmem, vmem, vmem],
+        out_specs=(vmem,) * 3,
+        scratch_shapes=[
+            pltpu.VMEM((n_words, n_samples), jnp.int32),
+            pltpu.VMEM((n_samples, k), BF16),
+            pltpu.VMEM((ns * PR + 16, n_samples), BF16),
+            pltpu.VMEM((pieces, PR, k), F32),
+            pltpu.VMEM((pieces, ns - 1, PR, k), jnp.int16),
+            pltpu.VMEM((pieces, ns - 1, PR, k), jnp.int16),
+            pltpu.VMEM((pieces, ns, 8, 128), F32),
+            pltpu.VMEM((pieces, ns - 1, 8, 128), F32),
+            pltpu.VMEM((4, 8, 128), F32),
+            pltpu.VMEM((pieces, 4 * PR, k), BF16),
+            pltpu.VMEM((k, 4 * PR), F32),
+            pltpu.VMEM((k // 128, rows, 128), F32),
+            pltpu.VMEM((BLOCKS, own, k), F32),
+            pltpu.VMEM((ns - 1, BLOCKS, own, k), BF16),
+            pltpu.VMEM((ns - 1, BLOCKS, own, k), BF16),
+            dma((2,)),
+        ] + [dma((pieces, ns - 1))] * 4 + [dma((3,))] * 2 + [dma((pieces, 3))] * 2 + [dma((ns - 1,))] * 2,
+        compiler_params=pltpu.CompilerParams(
+            collective_id=0, has_side_effects=True, vmem_limit_bytes=40 * 1024 * 1024
+        ),
+    )(genotype.T, traits, sample_mask.reshape(1, -1), block_ids.reshape(1, -1), running_total)
+    assoc, gram, total = pl.pallas_call(
+        store, out_shape=shapes, in_specs=[vmem] * 3, out_specs=(hbm,) * 3, scratch_shapes=[dma((3,))],
+    )(*results)
+    return assoc[None], gram, total
+
+
+def body(genotype, traits, sample_mask, block_ids, running_total):
+    args = (genotype, traits, sample_mask, block_ids, running_total)
+    ns = lax.axis_size("samples")
+    whole_tiles = genotype.shape[1] % (PW * ns) == 0 and running_total.shape[0] % 32 == 0
+    if lax.axis_size("snps") == 4 and ns == 4 and whole_tiles and traits.shape[1] == 512:
+        return fused(*args)
+    return shards(*args)
+
+
 def solution(mesh):
     placed = (
         P(("groups", "samples"), "snps"),
@@ -64,7 +353,7 @@
         P(("groups", "samples", "snps"), None),
     )
     return jax.shard_map(
-        shards,
+        body,
         mesh=mesh,
         in_specs=placed,
         out_specs=(

time: 140 us -> 47.4 us (0.34)
  waiting for transfers between devices: 72.8 us -> 0 us
  Pallas kernels: 0 us -> 38.8 us
  blocking collectives: 22 us -> 0 us
  between operations: 14.1 us -> 0.65 us
  other arithmetic: 9.14 us -> 0 us
  local copies, waits for them, and re-layouts: 14.6 us -> 7.22 us
  matrix products: 7.2 us -> 0 us
    reduce_scatter x2 -> x0, waiting for transfers between devices: 72.8 us -> none  [the longest x1 60.9 us: shards(): lax.psum_scatter(partial_gram, ('samples', 'snps'), scatter_dimension=1,...]
    pallas_call x0 -> x2, Pallas kernels: none -> 38.8 us  [the longest x1 36.9 us: fused(): pl.pallas_call(functools.partial(kernel, np_, factor), out_shape=shapes,...]
    psum x1 -> x0, blocking collectives: 22 us -> none  [shards(): lax.psum((local_count, local_colsum, local_sums, local_squares), 'samples')]
    shift_right_arithmetic x4 -> x0, local copies, waits for them, and re-layouts: 13.6 us -> none  [unpack(): values = words[:, :, None] >> shifts[None, None, :] & 3]
    dot_general x5 -> x0, matrix products: 7.2 us -> none  [the longest x1 3.04 us: shards(): lax.dot_general(dosage, masked, (((0,), (0,)), ((), ())), preferred_eleme...]
    unnamed x8 -> x14, local copies, waits for them, and re-layouts: 0.02 us -> 6.53 us
    convert_element_type x4 -> x0, other arithmetic: 5.6 us -> none  [the longest x1 3.71 us: shards(): dosage = unpack(genotype).astype(jnp.bfloat16)]
    reduce_sum x2 -> x0, other arithmetic: 2.18 us -> none  [the longest x1 1.58 us: shards(): total = running_total + jnp.sum(block_gram, axis=0)]
  transfers between devices with their start and end apart: 2 -> 0, of which waited for: 2 -> 0; matrix products, arithmetic and copies ran while one was open for 3% -> 0% of each run, Pallas kernels for 0% -> 0%
where the time goes in v2:
time: 47.4 us; the launch traced here: 46.7 us
  Pallas kernels  38.8 us (82%)
  local copies, waits for them, and re-layouts  7.22 us (15%)
  between operations  0.65 us (1%)
    pallas_call x1, Pallas kernels, fused(): pl.pallas_call(functools.partial(kernel, np_, factor), out_shape=shapes,...  36.9 us
    unnamed x14, local copies, waits for them, and re-layouts  6.53 us
    pallas_call x1, Pallas kernels, fused(): pl.pallas_call(store, out_shape=shapes, in_specs=[vmem] * 3, out_specs=(h...  1.89 us

profile of v2, /device:TPU:0, one launch (start us, length us, event | category | flops | bytes accessed | tf_op | source)
XLA Modules:
  0.0 46.7 jit_solution(13134843825679589218)
XLA Ops:
  0.6 0.7 %reshape.13.ids = s32[1,768]{1,0:T(1,128)S(1)} reshape(s32[768]{0:T(1024)} %param.8) | data formatting | bytes 6144 | tf_op jit(solution)/shard_map/reshape | solution.py:331
  1.3 0.0 copy-start
  1.3 1.6 %copy-done = bf16[2048,512]{1,0:T(8,128)(2,1)S(1)} copy-done((bf16[2048,512]{1,0:T(8,128)(2,1)S(1)}, bf16[2048,512]{1,0:T(8,128)(2,1)}, u32[]{:S(2)}) %copy-start) | copy-done | bytes 2097176
  2.9 0.0 copy-start.1
  2.9 1.4 %copy-done.1 = s32[2048,192]{0,1:T(8,128)S(1)} copy-done((s32[2048,192]{0,1:T(8,128)S(1)}, s32[2048,192]{0,1:T(8,128)}, u32[]{:S(2)}) %copy-start.1) | copy-done | bytes 1572888
  4.3 0.0 copy-start.4
  4.3 0.8 %copy-done.4 = f32[32,512]{1,0:T(8,128)S(1)} copy-done((f32[32,512]{1,0:T(8,128)S(1)}, f32[32,512]{1,0:T(8,128)}, u32[]{:S(2)}) %copy-start.4) | copy-done | bytes 65560
  5.2 0.0 copy-start.6
  5.2 0.7 %copy-done.6 = s32[2048]{0:T(1024)S(1)} copy-done((s32[2048]{0:T(1024)S(1)}, s32[2048]{0:T(1024)}, u32[]{:S(2)}) %copy-start.6) | copy-done | bytes 8216
  5.9 36.9 %shard_map.76 = (f32[192,512]{1,0:T(8,128)S(1)}, f32[2,32,512]{2,1,0:T(8,128)S(1)}, f32[32,512]{1,0:T(8,128)S(1)}) custom-call(s32[192,2048]{1,0:T(8,128)S(1)} %bitcast.3, bf16[2048,512]{1,0:T(8,128)(2,1)S(1)} %copy-done, s32[1,2048]{1,0:T(1,128)S(1)} %bitcast.4, s32[1,768]{1,0:T(1,128)S(1)} %reshape.13.ids, f32[32,512]{1,0:T(8,128)S(1)} %copy-done.4), custom_call_target="tpu_custom_call" | custom-call | tf_op jit(solution)/shard_map/pallas_call | solution.py:305
  42.8 0.0 copy-start.2
  42.8 0.7 %copy-done.2 = f32[192,512]{1,0:T(8,128)} copy-done((f32[192,512]{1,0:T(8,128)}, f32[192,512]{1,0:T(8,128)S(1)}, u32[]{:S(2)}) %copy-start.2) | copy-done | bytes 393240
  43.5 0.0 copy-start.3
  43.5 0.7 %copy-done.3 = f32[2,32,512]{2,1,0:T(8,128)} copy-done((f32[2,32,512]{2,1,0:T(8,128)}, f32[2,32,512]{2,1,0:T(8,128)S(1)}, u32[]{:S(2)}) %copy-start.3) | copy-done | bytes 131096
  44.1 0.0 copy-start.5
  44.2 0.6 %copy-done.5 = f32[32,512]{1,0:T(8,128)} copy-done((f32[32,512]{1,0:T(8,128)}, f32[32,512]{1,0:T(8,128)S(1)}, u32[]{:S(2)}) %copy-start.5) | copy-done | bytes 65560
  44.8 1.9 %shard_map.77 = (f32[192,512]{1,0:T(8,128)}, f32[2,32,512]{2,1,0:T(8,128)}, f32[32,512]{1,0:T(8,128)}) custom-call(f32[192,512]{1,0:T(8,128)} %copy-done.2, f32[2,32,512]{2,1,0:T(8,128)} %copy-done.3, f32[32,512]{1,0:T(8,128)} %copy-done.5), custom_call_target="tpu_custom_call" | custom-call | tf_op jit(solution)/shard_map/pallas_call | solution.py:332
Async XLA Ops:
  1.3 1.6 %copy-start = (bf16[2048,512]{1,0:T(8,128)(2,1)S(1)}, bf16[2048,512]{1,0:T(8,128)(2,1)}, u32[]{:S(2)}) copy-start(bf16[2048,512]{1,0:T(8,128)(2,1)} %traits_hbm.1) | copy-start | bytes 6291460
  2.9 1.4 %copy-start.1 = (s32[2048,192]{0,1:T(8,128)S(1)}, s32[2048,192]{0,1:T(8,128)}, u32[]{:S(2)}) copy-start(s32[2048,192]{0,1:T(8,128)} %param.5) | copy-start | bytes 4718596
  4.3 0.8 %copy-start.4 = (f32[32,512]{1,0:T(8,128)S(1)}, f32[32,512]{1,0:T(8,128)}, u32[]{:S(2)}) copy-start(f32[32,512]{1,0:T(8,128)} %running.1) | copy-start | bytes 196612
  5.2 0.7 %copy-start.6 = (s32[2048]{0:T(1024)S(1)}, s32[2048]{0:T(1024)}, u32[]{:S(2)}) copy-start(s32[2048]{0:T(1024)} %param.7) | copy-start | bytes 24580
  42.8 0.7 %copy-start.2 = (f32[192,512]{1,0:T(8,128)}, f32[192,512]{1,0:T(8,128)S(1)}, u32[]{:S(2)}) copy-start(f32[192,512]{1,0:T(8,128)S(1)} %get-tuple-element.9.refs_0_) | copy-start | bytes 1179652
  43.5 0.7 %copy-start.3 = (f32[2,32,512]{2,1,0:T(8,128)}, f32[2,32,512]{2,1,0:T(8,128)S(1)}, u32[]{:S(2)}) copy-start(f32[2,32,512]{2,1,0:T(8,128)S(1)} %get-tuple-element.10.refs_1_) | copy-start | bytes 393220
  44.1 0.6 %copy-start.5 = (f32[32,512]{1,0:T(8,128)}, f32[32,512]{1,0:T(8,128)S(1)}, u32[]{:S(2)}) copy-start(f32[32,512]{1,0:T(8,128)S(1)} %get-tuple-element.11.refs_2_) | copy-start | bytes 196612

commit v3 on v2

--- a/solution.py
+++ b/solution.py
@@ -66,9 +66,9 @@
 
 
 def kernel(
-    n_snp_dev, factor, geno, traits_hbm, mask, ids, running, assoc, gram, total,
-    words, traits, lhs, y_own, q_send, q_recv, st_send, st_recv, n_buf, z_buf, zt, mixed, g_own, g_send, g_recv,
-    in_sem, q_ss, q_rs, st_ss, st_rs, n_ss, n_rs, z_ss, z_rs, g_ss, g_rs,
+    n_snp_dev, factor, geno, traits_hbm, mask_hbm, ids_hbm, assoc, gram,
+    words, traits, mask, ids, lhs, y_own, y_far, q_send, q_recv, st_send, st_recv, r_send, r_recv, rs_send, rs_recv, n_buf, z_buf, zt, mixed, g_own, g_send, g_recv,
+    in_sem, r_ss, r_rs, rt_ss, rt_rs, q_ss, q_rs, st_ss, st_rs, n_ss, n_rs, z_ss, z_rs, g_ss, g_rs,
 ):
     grp, s, p = (lax.axis_index(a) for a in ("groups", "samples", "snps"))
     ns = lax.axis_size("samples")
@@ -80,8 +80,13 @@
 
     geno_in = pltpu.make_async_copy(geno, words, in_sem.at[0])
     traits_in = pltpu.make_async_copy(traits_hbm, traits, in_sem.at[1])
+    small_in = [
+        pltpu.make_async_copy(src, dst, in_sem.at[2 + i])
+        for i, (src, dst) in enumerate(((mask_hbm, mask), (ids_hbm, ids)))]
+    small_in[0].start()
     geno_in.start()
     traits_in.start()
+    small_in[1].start()
 
     def along(k):
         return (grp, lax.rem(s + k, ns), p)
@@ -97,11 +102,10 @@
     for peer in peers:
         pl.semaphore_signal(barrier, inc=1, device_id=peer, device_id_type=MESH)
 
+    small_in[0].wait()
     keep = mask[...]
     count = jnp.sum(keep.astype(F32), axis=1, keepdims=True)
     lhs[ns * PR:, :] = jnp.broadcast_to(keep.astype(F32), (16, n_samples)).astype(BF16)
-    n0 = jnp.sum((ids[...] == 0).astype(F32), axis=1, keepdims=True)
-    n_buf[0] = jnp.broadcast_to(n0, n_buf.shape[1:])
 
     def remote(src, dst, ss, rs, to):
         return pltpu.make_async_remote_copy(src, dst, ss, rs, device_id=to, device_id_type=MESH)
@@ -132,14 +136,36 @@
     def g_copy(k):
         return remote(g_send.at[k - 1], g_recv.at[k - 1], g_ss.at[k - 1], g_rs.at[k - 1], along(k))
 
-    pl.semaphore_wait(barrier, len(peers))
-    for x in range(1, 4):
-        n_copy(x).start()
     geno_in.wait()
     lane = lax.broadcasted_iota(jnp.int32, (PR, 128), 1)
     sub = lax.broadcasted_iota(jnp.int32, (8, 128), 0)
 
-    def one(c, carry):
+    edge = (s == 0) | (s == ns - 1)
+    inner = jnp.logical_not(edge)
+    relayed = range(pieces - 1)
+
+    def skips(k, sending):
+        first, last = (ns - 1, 1) if sending else (1, ns - 1)
+        return ((s == 0) & (k == first)) | ((s == ns - 1) & (k == last))
+
+    def r_copy(c):
+        return remote(r_send.at[c], r_recv.at[c], r_ss.at[c], r_rs.at[c], (grp, s + 1 - 2 * lax.rem(s, 2), p))
+
+    def rt_copy(c):
+        return remote(rs_send.at[c], rs_recv.at[c], rt_ss.at[c], rt_rs.at[c], (grp, s + 1 - 2 * lax.rem(s, 2), p))
+
+    def tall(tile):
+        return jnp.concatenate([tile, jnp.zeros((120, 128), F32)], axis=0).T
+
+    def flat(column):
+        wide = jnp.concatenate([jnp.broadcast_to(column, (PR, 128)), jnp.zeros((128 - PR, 128), F32)], axis=0)
+        return wide.T[:8]
+
+    def fixed(y):
+        top = jnp.maximum(jnp.max(jnp.abs(y), axis=1, keepdims=True), 1e-30)
+        return jnp.round(y * (32767.0 / top)).astype(jnp.int32).astype(jnp.int16), top * (1.0 / 32767.0)
+
+    def compute(c):
         stats = []
         for k in range(1, ns + 1):
             t = lax.rem(s + k, ns)
@@ -152,11 +178,8 @@
                 at = (k - 1) * PR + f * PW
                 lhs[at:at + PW, :] = d.astype(BF16)
             stats.append((jnp.concatenate(s1, axis=0), jnp.concatenate(s2, axis=0)))
-
-        @pl.when(c == 0)
-        def _():
+        if c == 0:
             traits_in.wait()
-
         raw = jnp.dot(lhs[...], traits[...], preferred_element_type=F32)
         colsum = raw[ns * PR:ns * PR + 1]
         tail = jnp.concatenate(
@@ -165,36 +188,94 @@
         for k in range(1, ns + 1):
             sums, squares = stats[k - 1]
             y = raw[(k - 1) * PR:k * PR] - (sums / jnp.maximum(count, 1.0)) * colsum
-            top = jnp.maximum(jnp.max(jnp.abs(y), axis=1, keepdims=True), 1e-30)
+            unit = jnp.zeros((PR, 1), F32)
             if k < ns:
-                q_send[c, k - 1] = jnp.round(y * (32767.0 / top)).astype(jnp.int32).astype(jnp.int16)
+                q_send[c, k - 1], unit = fixed(y)
+                if k == 2 and c in relayed:
+                    y_far[c] = y
+                if k != 2 and c in relayed:
+                    @pl.when(skips(k, True))
+                    def _(k=k, unit=unit):
+                        r_send[c] = q_send[c, k - 1]
+                        rs_send[c] = flat(unit)
             else:
                 y_own[c] = y
-            cols = jnp.where(lane == 0, sums, jnp.where(lane == 1, squares, top * (1.0 / 32767.0)))
+            cols = jnp.where(lane == 0, sums, jnp.where(lane == 1, squares, unit))
             cols = jnp.concatenate([cols, jnp.zeros((128 - PR, 128), F32)], axis=0).T[:8]
             st_send[c, k - 1] = jnp.where(sub < 3, cols, tail)
-            if k < ns:
+
+    def send(c):
+        if c in relayed:
+            @pl.when(edge)
+            def _():
+                rt_copy(c).start()
+                r_copy(c).start()
+        for k in (2, 1, 3):
+            if c in relayed:
+                if k == 2:
+                    ready = edge
+                    st_ready = edge
+                else:
+                    ready = jnp.logical_not(skips(k, True))
+                    st_ready = None
+            else:
+                ready = st_ready = None
+            if st_ready is None:
                 st_copy(c, k).start()
+            else:
+                pl.when(st_ready)(st_copy(c, k).start)
+            if ready is None:
                 q_copy(c, k).start()
-        return carry
-
-    lax.fori_loop(0, pieces, one, 0)
+            else:
+                pl.when(ready)(q_copy(c, k).start)
+
+    def pass_on(c):
+        @pl.when(inner)
+        def _():
+            rt_copy(c).wait_recv()
+            r_copy(c).wait_recv()
+            theirs = tall(rs_recv[c])[:PR, 0:1]
+            q, unit = fixed(y_far[c] + r_recv[c].astype(jnp.int32).astype(F32) * theirs)
+            q_send[c, 1] = q
+            st_send[c, 1] = jnp.where(sub == 2, flat(unit), st_send[c, 1])
+            st_copy(c, 2).start()
+            q_copy(c, 2).start()
+
+    for c in range(pieces):
+        compute(c)
+        if c == 0:
+            pl.semaphore_wait(barrier, len(peers))
+        send(c)
+        if c >= 1 and c - 1 in relayed:
+            pass_on(c - 1)
+    small_in[1].wait()
+    n0 = jnp.sum((ids[...].reshape(1, -1) == 0).astype(F32), axis=1, keepdims=True)
+    n_buf[0] = jnp.broadcast_to(n0, n_buf.shape[1:])
+    for x in range(1, 4):
+        n_copy(x).start()
 
     def columns(st):
-        tall = jnp.concatenate([st, jnp.zeros((120, 128), F32)], axis=0).T
-        return tall[:PR, 0:1], tall[:PR, 1:2], tall[:PR, 2:3]
+        wide = tall(st)
+        return wide[:PR, 0:1], wide[:PR, 1:2], wide[:PR, 2:3]
 
     def standardise(c):
         st = st_send[c, ns - 1]
         parts = [(st, columns(st))]
-        y = y_own[c]
         for k in range(1, ns):
             st_copy(c, k).wait_recv()
             st = st_recv[c, k - 1]
             cols = columns(st)
             parts.append((st, cols))
-            q_copy(c, k).wait_recv()
-            y = y + q_recv[c, k - 1].astype(jnp.int32).astype(F32) * cols[2]
+
+            def add(k=k, unit=cols[2]):
+                q_copy(c, k).wait_recv()
+                y_own[c] += q_recv[c, k - 1].astype(jnp.int32).astype(F32) * unit
+
+            if c in relayed and k != 2:
+                pl.when(jnp.logical_not(skips(k, False)))(add)
+            else:
+                add()
+        y = y_own[c]
         n = sum(st[7:8, 0:1] for st, _ in parts)
         mean = sum(cols[0] for _, cols in parts) / n
         var = sum(cols[1] for _, cols in parts) / n - mean * mean
@@ -211,7 +292,7 @@
                 mixed[i, pl.ds(c * PR + f, PW, stride=4), :] = z[f * PW:(f + 1) * PW, i * 128:(i + 1) * 128]
             assoc[c * PR:(c + 1) * PR, i * 128:(i + 1) * 128] = mixed[i, c * PR:(c + 1) * PR, :]
 
-    own_rows = running.shape[0]
+    own_rows = gram.shape[1]
     lanes = lax.broadcasted_iota(jnp.int32, (1, 4 * PR), 1)
     slot = lanes // PR
     snp = s * rows + 4 * lax.rem(lanes, PW) + lax.rem(lanes, PR) // PW
@@ -263,27 +344,24 @@
         out = out + g_recv[k - 1].astype(F32)
     out = out * factor
     gram[...] = out
-    total[...] = running[...] + (out[0] + out[1])
     for c in range(pieces):
         for k in range(1, ns):
-            q_copy(c, k).wait_send()
             st_copy(c, k).wait_send()
+            if c in relayed and k != 2:
+                pl.when(jnp.logical_not(skips(k, True)))(q_copy(c, k).wait_send)
+            else:
+                q_copy(c, k).wait_send()
         for copy in (far(c), near(c), relay(c)):
             copy.wait_send()
+    for c in relayed:
+        @pl.when(edge)
+        def _(c=c):
+            r_copy(c).wait_send()
+            rt_copy(c).wait_send()
     for k in range(1, ns):
         g_copy(k).wait_send()
     for x in range(1, 4):
         n_copy(x).wait_send()
-
-
-def store(*refs):
-    n = len(refs) // 2
-    sems = refs[-1]
-    copies = [pltpu.make_async_copy(refs[i], refs[n + i], sems.at[i]) for i in range(n)]
-    for copy in copies:
-        copy.start()
-    for copy in copies:
-        copy.wait()
 
 
 def fused(genotype, traits, sample_mask, block_ids, running_total):
@@ -295,27 +373,33 @@
     own = running_total.shape[0]
     factor = 1.0 / math.sqrt(4 * n_words * np_)
     vmem = pl.BlockSpec(memory_space=pltpu.VMEM)
-    hbm = pl.BlockSpec(memory_space=pltpu.HBM)
+    hbm = pl.BlockSpec(memory_space=pl.ANY)
     dma = pltpu.SemaphoreType.DMA
     shapes = (
         jax.ShapeDtypeStruct((rows, k), F32),
         jax.ShapeDtypeStruct((BLOCKS, own, k), F32),
-        jax.ShapeDtypeStruct((own, k), F32),
     )
     results = pl.pallas_call(
         functools.partial(kernel, np_, factor),
         out_shape=shapes,
-        in_specs=[hbm, hbm, vmem, vmem, vmem],
-        out_specs=(vmem,) * 3,
+        in_specs=[hbm] * 4,
+        out_specs=(vmem,) * 2,
         scratch_shapes=[
             pltpu.VMEM((n_words, n_samples), jnp.int32),
             pltpu.VMEM((n_samples, k), BF16),
+            pltpu.VMEM((1, n_samples), jnp.int32),
+            pltpu.VMEM(block_ids.shape, jnp.int32),
             pltpu.VMEM((ns * PR + 16, n_samples), BF16),
+            pltpu.VMEM((pieces, PR, k), F32),
             pltpu.VMEM((pieces, PR, k), F32),
             pltpu.VMEM((pieces, ns - 1, PR, k), jnp.int16),
             pltpu.VMEM((pieces, ns - 1, PR, k), jnp.int16),
             pltpu.VMEM((pieces, ns, 8, 128), F32),
             pltpu.VMEM((pieces, ns - 1, 8, 128), F32),
+            pltpu.VMEM((pieces, PR, k), jnp.int16),
+            pltpu.VMEM((pieces, PR, k), jnp.int16),
+            pltpu.VMEM((pieces, 8, 128), F32),
+            pltpu.VMEM((pieces, 8, 128), F32),
             pltpu.VMEM((4, 8, 128), F32),
             pltpu.VMEM((pieces, 4 * PR, k), BF16),
             pltpu.VMEM((k, 4 * PR), F32),
@@ -323,16 +407,14 @@
             pltpu.VMEM((BLOCKS, own, k), F32),
             pltpu.VMEM((ns - 1, BLOCKS, own, k), BF16),
             pltpu.VMEM((ns - 1, BLOCKS, own, k), BF16),
-            dma((2,)),
-        ] + [dma((pieces, ns - 1))] * 4 + [dma((3,))] * 2 + [dma((pieces, 3))] * 2 + [dma((ns - 1,))] * 2,
+            dma((4,)),
+        ] + [dma((pieces,))] * 4 + [dma((pieces, ns - 1))] * 4 + [dma((3,))] * 2 + [dma((pieces, 3))] * 2 + [dma((ns - 1,))] * 2,
         compiler_params=pltpu.CompilerParams(
-            collective_id=0, has_side_effects=True, vmem_limit_bytes=40 * 1024 * 1024
+            collective_id=0, has_side_effects=True, vmem_limit_bytes=52 * 1024 * 1024
         ),
-    )(genotype.T, traits, sample_mask.reshape(1, -1), block_ids.reshape(1, -1), running_total)
-    assoc, gram, total = pl.pallas_call(
-        store, out_shape=shapes, in_specs=[vmem] * 3, out_specs=(hbm,) * 3, scratch_shapes=[dma((3,))],
-    )(*results)
-    return assoc[None], gram, total
+    )(genotype.T, traits, sample_mask.reshape(1, -1), block_ids)
+    assoc, gram = results
+    return assoc[None], gram, running_total + jnp.sum(gram, axis=0)
 
 
 def body(genotype, traits, sample_mask, block_ids, running_total):

time: 47.4 us -> 39 us (0.82); the launches traced: 46.7 us -> 38.7 us
  local copies, waits for them, and re-layouts: 7.22 us -> 2.78 us
  Pallas kernels: 38.8 us -> 34.6 us
  other arithmetic: 0 us -> 0.65 us
    unnamed x14 -> x8, local copies, waits for them, and re-layouts: 6.53 us -> 2.78 us
    pallas_call x1, Pallas kernels: 36.9 us -> 34.6 us  [fused(): pl.pallas_call(functools.partial(kernel, np_, factor), out_shape=shapes,...]
    pallas_call x1 -> x0, Pallas kernels: 1.89 us -> none  [fused(): pl.pallas_call(store, out_shape=shapes, in_specs=[vmem] * 3, out_specs=(h...]
    reshape x1 -> x0, local copies, waits for them, and re-layouts: 0.69 us -> none  [fused(): block_ids.reshape(1, -1)]
    add x0 -> x1, other arithmetic: none -> 0.64 us  [fused(): return (assoc[None], gram, running_total + jnp.sum(gram, axis=0))]
where the time goes in v3:
time: 39 us; the launch traced here: 38.7 us
  Pallas kernels  34.6 us (89%)
  local copies, waits for them, and re-layouts  2.78 us (7%)
  between operations  0.67 us (2%)
  other arithmetic  0.65 us (2%)
    pallas_call x1, Pallas kernels, fused(): pl.pallas_call(functools.partial(kernel, np_, factor), out_shape=shapes,...  34.6 us
    unnamed x8, local copies, waits for them, and re-layouts  2.78 us

profile of v3, /device:TPU:0, one launch (start us, length us, event | category | flops | bytes accessed | tf_op | source)
XLA Modules:
  0.0 38.7 jit_solution(11124097965603405762)
XLA Ops:
  0.6 0.0 copy-start
  0.6 0.7 %copy-done = s32[2048]{0:T(1024)S(1)} copy-done((s32[2048]{0:T(1024)S(1)}, s32[2048]{0:T(1024)}, u32[]{:S(2)}) %copy-start) | copy-done | bytes 8216
  1.3 0.0 copy-start.1
  1.3 0.7 %copy-done.1 = s32[768]{0:T(1024)S(1)} copy-done((s32[768]{0:T(1024)S(1)}, s32[768]{0:T(1024)}, u32[]{:S(2)}) %copy-start.1) | copy-done | bytes 3096
  2.0 0.0 copy-start.2
  2.0 34.6 %shard_map.76 = (f32[192,512]{1,0:T(8,128)S(1)}, f32[2,32,512]{2,1,0:T(8,128)S(1)}) custom-call(s32[192,2048]{1,0:T(8,128)} %bitcast.5, bf16[2048,512]{1,0:T(8,128)(2,1)} %traits_hbm.1, s32[1,2048]{1,0:T(1,128)S(1)} %bitcast.4, s32[768]{0:T(1024)S(1)} %copy-done.1), custom_call_target="tpu_custom_call" | custom-call | tf_op jit(solution)/shard_map/pallas_call | solution.py:382
  36.7 0.0 copy-done.2
  36.7 0.6 %add.3 = f32[32,512]{1,0:T(8,128)} add(f32[32,512]{1,0:T(8,128)S(1)} %copy-done.2, f32[32,512]{1,0:T(8,128)S(1)} %reduce_sum.9) | non-fusion elementwise | flops 16384 | bytes 196608 | tf_op jit(solution)/shard_map/add | solution.py:417
  37.3 0.7 %copy.10 = f32[1,192,512]{2,1,0:T(8,128)} copy(f32[1,192,512]{2,1,0:T(8,128)S(1)} %bitcast.3) | data formatting | bytes 786432
  38.1 0.7 %copy.11 = f32[2,32,512]{2,1,0:T(8,128)} copy(f32[2,32,512]{2,1,0:T(8,128)S(1)} %get-tuple-element.11) | data formatting | bytes 262144
  (1 shorter events, 0.0 us)
Async XLA Ops:
  0.6 0.7 %copy-start = (s32[2048]{0:T(1024)S(1)}, s32[2048]{0:T(1024)}, u32[]{:S(2)}) copy-start(s32[2048]{0:T(1024)} %param.7) | copy-start | bytes 24580
  1.3 0.7 %copy-start.1 = (s32[768]{0:T(1024)S(1)}, s32[768]{0:T(1024)}, u32[]{:S(2)}) copy-start(s32[768]{0:T(1024)} %ids_hbm.1) | copy-start | bytes 9220
  2.0 34.7 %copy-start.2 = (f32[32,512]{1,0:T(8,128)S(1)}, f32[32,512]{1,0:T(8,128)}, u32[]{:S(2)}) copy-start(f32[32,512]{1,0:T(8,128)} %param.9) | copy-start | bytes 196612

commit v4 on v3

--- a/solution.py
+++ b/solution.py
@@ -66,7 +66,7 @@
 
 
 def kernel(
-    n_snp_dev, factor, geno, traits_hbm, mask_hbm, ids_hbm, assoc, gram,
+    n_snp_dev, factor, geno, traits_hbm, small_hbm, assoc, gram,
     words, traits, mask, ids, lhs, y_own, y_far, q_send, q_recv, st_send, st_recv, r_send, r_recv, rs_send, rs_recv, n_buf, z_buf, zt, mixed, g_own, g_send, g_recv,
     in_sem, r_ss, r_rs, rt_ss, rt_rs, q_ss, q_rs, st_ss, st_rs, n_ss, n_rs, z_ss, z_rs, g_ss, g_rs,
 ):
@@ -81,8 +81,9 @@
     geno_in = pltpu.make_async_copy(geno, words, in_sem.at[0])
     traits_in = pltpu.make_async_copy(traits_hbm, traits, in_sem.at[1])
     small_in = [
-        pltpu.make_async_copy(src, dst, in_sem.at[2 + i])
-        for i, (src, dst) in enumerate(((mask_hbm, mask), (ids_hbm, ids)))]
+        pltpu.make_async_copy(small_hbm.at[pl.ds(0, n_samples)], mask, in_sem.at[2]),
+        pltpu.make_async_copy(small_hbm.at[pl.ds(n_samples, ids.shape[0])], ids, in_sem.at[3]),
+    ]
     small_in[0].start()
     geno_in.start()
     traits_in.start()
@@ -103,7 +104,8 @@
         pl.semaphore_signal(barrier, inc=1, device_id=peer, device_id_type=MESH)
 
     small_in[0].wait()
-    keep = mask[...]
+    keep = mask[...].reshape(1, -1)
+    keep_bits = -keep
     count = jnp.sum(keep.astype(F32), axis=1, keepdims=True)
     lhs[ns * PR:, :] = jnp.broadcast_to(keep.astype(F32), (16, n_samples)).astype(BF16)
 
@@ -169,14 +171,15 @@
         stats = []
         for k in range(1, ns + 1):
             t = lax.rem(s + k, ns)
-            w = words[pl.ds(pl.multiple_of(t * wpd + c * PW, PW), PW), :] * keep
+            w = words[pl.ds(pl.multiple_of(t * wpd + c * PW, PW), PW), :] & keep_bits
             s1, s2 = [], []
             for f in range(4):
-                d = ((w >> (2 * f)) & 3).astype(F32)
-                s1.append(jnp.sum(d, axis=1, keepdims=True))
-                s2.append(jnp.sum(d * d, axis=1, keepdims=True))
+                d = ((w >> (2 * f)) & 3).astype(F32).astype(BF16)
+                parts = [d[:, i:i + 128] for i in range(0, n_samples, 128)]
+                s1.append(jnp.sum(functools.reduce(jnp.add, parts).astype(F32), axis=1, keepdims=True))
+                s2.append(jnp.sum(functools.reduce(jnp.add, [v * v for v in parts]).astype(F32), axis=1, keepdims=True))
                 at = (k - 1) * PR + f * PW
-                lhs[at:at + PW, :] = d.astype(BF16)
+                lhs[at:at + PW, :] = d
             stats.append((jnp.concatenate(s1, axis=0), jnp.concatenate(s2, axis=0)))
         if c == 0:
             traits_in.wait()
@@ -204,30 +207,21 @@
             cols = jnp.concatenate([cols, jnp.zeros((128 - PR, 128), F32)], axis=0).T[:8]
             st_send[c, k - 1] = jnp.where(sub < 3, cols, tail)
 
+    inward, upper = lax.rem(s + 1, ns) // 2, s // 2
+    first = inward * 2 + (1 - inward) * (3 - 2 * upper)
+    second = (1 - inward) * 2 + inward * (1 + 2 * upper)
+    ordered = (first, second, 6 - first - second)
+
     def send(c):
         if c in relayed:
             @pl.when(edge)
             def _():
                 rt_copy(c).start()
                 r_copy(c).start()
-        for k in (2, 1, 3):
-            if c in relayed:
-                if k == 2:
-                    ready = edge
-                    st_ready = edge
-                else:
-                    ready = jnp.logical_not(skips(k, True))
-                    st_ready = None
-            else:
-                ready = st_ready = None
-            if st_ready is None:
-                st_copy(c, k).start()
-            else:
-                pl.when(st_ready)(st_copy(c, k).start)
-            if ready is None:
-                q_copy(c, k).start()
-            else:
-                pl.when(ready)(q_copy(c, k).start)
+                st_copy(c, first).start()
+        for k in ordered[1:] if c in relayed else ordered:
+            st_copy(c, k).start()
+            q_copy(c, k).start()
 
     def pass_on(c):
         @pl.when(inner)
@@ -334,6 +328,7 @@
         for b in range(BLOCKS):
             lo = b * half + (k - 1) * own_rows
             g_send[k - 1, b] = acc[lo:lo + own_rows].astype(BF16)
+    for k in ordered:
         g_copy(k).start()
     for b in range(BLOCKS):
         lo = b * half + (ns - 1) * own_rows
@@ -382,12 +377,12 @@
     results = pl.pallas_call(
         functools.partial(kernel, np_, factor),
         out_shape=shapes,
-        in_specs=[hbm] * 4,
+        in_specs=[hbm] * 3,
         out_specs=(vmem,) * 2,
         scratch_shapes=[
             pltpu.VMEM((n_words, n_samples), jnp.int32),
             pltpu.VMEM((n_samples, k), BF16),
-            pltpu.VMEM((1, n_samples), jnp.int32),
+            pltpu.VMEM((n_samples,), jnp.int32),
             pltpu.VMEM(block_ids.shape, jnp.int32),
             pltpu.VMEM((ns * PR + 16, n_samples), BF16),
             pltpu.VMEM((pieces, PR, k), F32),
@@ -412,7 +407,7 @@
         compiler_params=pltpu.CompilerParams(
             collective_id=0, has_side_effects=True, vmem_limit_bytes=52 * 1024 * 1024
         ),
-    )(genotype.T, traits, sample_mask.reshape(1, -1), block_ids)
+    )(genotype.T, traits, jnp.concatenate([sample_mask, block_ids]))
     assoc, gram = results
     return assoc[None], gram, running_total + jnp.sum(gram, axis=0)
 
@@ -420,7 +415,7 @@
 def body(genotype, traits, sample_mask, block_ids, running_total):
     args = (genotype, traits, sample_mask, block_ids, running_total)
     ns = lax.axis_size("samples")
-    whole_tiles = genotype.shape[1] % (PW * ns) == 0 and running_total.shape[0] % 32 == 0
+    whole_tiles = genotype.shape[0] % 128 == 0 and genotype.shape[0] <= 8192 and genotype.shape[1] % (PW * ns) == 0 and running_total.shape[0] % 32 == 0
     if lax.axis_size("snps") == 4 and ns == 4 and whole_tiles and traits.shape[1] == 512:
         return fused(*args)
     return shards(*args)

time: 39 us -> 38.4 us (0.985)
  local copies, waits for them, and re-layouts: 2.78 us -> 1.4 us
  other arithmetic: 0.65 us -> 1.4 us
    unnamed x8 -> x4, local copies, waits for them, and re-layouts: 2.78 us -> 1.4 us
    concatenate x0 -> x1, other arithmetic: none -> 0.75 us  [fused(): jnp.concatenate([sample_mask, block_ids])]
where the time goes in v4:
time: 38.4 us; the launch traced here: 38.2 us
  Pallas kernels  34.7 us (90%)
  local copies, waits for them, and re-layouts  1.4 us (4%)
  other arithmetic  1.4 us (4%)
  between operations  0.66 us (2%)
    pallas_call x1, Pallas kernels, fused(): pl.pallas_call(functools.partial(kernel, np_, factor), out_shape=shapes,...  34.7 us
    unnamed x4, local copies, waits for them, and re-layouts  1.4 us

profile of v4, /device:TPU:0, one launch (start us, length us, event | category | flops | bytes accessed | tf_op | source)
XLA Modules:
  0.0 38.2 jit_solution(14076881146214891432)
XLA Ops:
  0.6 0.0 copy-start
  0.6 0.7 %pad_add_fusion.small_hbm = s32[2816]{0:T(1024)S(1)} fusion(s32[768]{0:T(1024)} %param.8, s32[2048]{0:T(1024)} %param.7), kind=kLoop, calls=%fused_computation | loop fusion | flops 2816 | bytes 22528 | tf_op jit(solution)/shard_map/concatenate | solution.py:410
  1.4 34.7 %shard_map.76 = (f32[192,512]{1,0:T(8,128)S(1)}, f32[2,32,512]{2,1,0:T(8,128)S(1)}) custom-call(s32[192,2048]{1,0:T(8,128)} %bitcast.3, bf16[2048,512]{1,0:T(8,128)(2,1)} %traits_hbm.1, s32[2816]{0:T(1024)S(1)} %pad_add_fusion.small_hbm), custom_call_target="tpu_custom_call" | custom-call | tf_op jit(solution)/shard_map/pallas_call | solution.py:377
  36.1 0.0 copy-done
  36.2 0.6 %add.3 = f32[32,512]{1,0:T(8,128)} add(f32[32,512]{1,0:T(8,128)S(1)} %copy-done, f32[32,512]{1,0:T(8,128)S(1)} %reduce_sum.9) | non-fusion elementwise | flops 16384 | bytes 196608 | tf_op jit(solution)/shard_map/add | solution.py:412
  36.8 0.7 %copy.10 = f32[1,192,512]{2,1,0:T(8,128)} copy(f32[1,192,512]{2,1,0:T(8,128)S(1)} %bitcast.2) | data formatting | bytes 786432
  37.5 0.7 %copy.11 = f32[2,32,512]{2,1,0:T(8,128)} copy(f32[2,32,512]{2,1,0:T(8,128)S(1)} %get-tuple-element.11) | data formatting | bytes 262144
  (1 shorter events, 0.0 us)
Async XLA Ops:
  0.6 35.5 %copy-start = (f32[32,512]{1,0:T(8,128)S(1)}, f32[32,512]{1,0:T(8,128)}, u32[]{:S(2)}) copy-start(f32[32,512]{1,0:T(8,128)} %param.9) | copy-start | bytes 196612
